TPU v7x, 32 devices: a whole 2x2x4 slice. The times are simulated.
32 devices in a mesh: groups: 1, row: 32 (over z, y, x, core), col: 1.
Axes of the slice: x: 2, y: 2, z: 4, core: 2. Of those that a mesh axis runs over, the one named last changes fastest.
Arguments:
- features_in: bfloat16 [64, 128, 128], P(None, ('groups', 'row'), 'col'), may hold values from -6 to 6
- gain_outer: float32 [8, 64], replicated, may hold values from 0.25 to 1.75
- bias_outer: float32 [8, 64], replicated, may hold values from -3 to 3
- w_narrow: bfloat16 [8, 32, 576], replicated, may hold values from -0.25 to 0.25
- gain_inner: float32 [8, 32], replicated, may hold values from 0.25 to 1.75
- bias_inner: float32 [8, 32], replicated, may hold values from -3 to 3
- w_widen: bfloat16 [8, 64, 288], replicated, may hold values from -0.375 to 0.375
Outputs:
- features_out: bfloat16 [64, 128, 128], P(None, ('groups', 'row'), 'col')
All inputs are finite; a program needn't handle non-finite values.
Results may differ from a plain program's by a relative error of at most 0.022.
Values may be sent and summed in bfloat16 or wider, within the bound.
A program may use at most 64 MiB of HBM per device.

v0:
```python
import jax
import jax.numpy as jnp
from jax import lax
from jax.sharding import PartitionSpec as P


def padded_2(block, sides, width):
    for axis, dim in sides:
        count = lax.axis_size(axis)
        forward = [(i, i + 1) for i in range(count - 1)]
        backward = [(target, source) for source, target in forward]
        low = lax.ppermute(
            lax.slice_in_dim(block, block.shape[dim] - width, None, axis=dim), axis, forward
        )
        high = lax.ppermute(lax.slice_in_dim(block, 0, width, axis=dim), axis, backward)
        block = jnp.concatenate([low, block, high], axis=dim)
    return block


def dilated_taps(padded, weight, dilation, rows, cols):
    channels = padded.shape[0]
    total = None
    for vertical in range(3):
        for lateral in range(3):
            tap_index = vertical * 3 + lateral
            window = padded[
                :,
                vertical * dilation : vertical * dilation + rows,
                lateral * dilation : lateral * dilation + cols,
            ]
            weight_tap = weight[:, tap_index * channels : (tap_index + 1) * channels]
            term = jnp.einsum("oc,crw->orw", weight_tap, window, preferred_element_type=jnp.float32)
            total = term if total is None else total + term
    return total


def mirrored(stream):
    channels = stream.shape[0]
    rows = stream.shape[1]
    width = stream.shape[2]
    row_count = lax.axis_size("row")
    core_count = lax.axis_size("col")
    squares = stream.reshape(channels, rows, row_count, core_count, rows)
    outgoing = squares.transpose(3, 2, 4, 1, 0).reshape(
        core_count, row_count, rows * rows * channels
    )
    received = lax.all_to_all(
        lax.all_to_all(outgoing, "row", split_axis=1, concat_axis=1, tiled=True),
        "col",
        split_axis=0,
        concat_axis=0,
        tiled=True,
    )
    partner = (
        received.reshape(core_count, row_count, rows, rows, channels)
        .transpose(4, 2, 1, 0, 3)
        .reshape(channels, rows, width)
    )
    return ((stream.astype(jnp.float32) + partner.astype(jnp.float32)) * 0.5).astype(jnp.bfloat16)


def averaged_tiles(stream):
    strips = lax.all_to_all(stream, "col", split_axis=1, concat_axis=2, tiled=True)
    merged = mirrored(strips)
    return lax.all_to_all(merged, "col", split_axis=2, concat_axis=1, tiled=True)


def inside_mask(row_start, col_start, offset, row_count, col_count, side):
    global_rows = row_start - offset + lax.iota(jnp.int32, row_count)
    global_cols = col_start - offset + lax.iota(jnp.int32, col_count)
    rows_ok = (global_rows >= 0) & (global_rows < side)
    cols_ok = (global_cols >= 0) & (global_cols < side)
    return (rows_ok[:, None] & cols_ok[None, :])[None]


def body(features_in, gain_outer, bias_outer, w_narrow, gain_inner, bias_inner, w_widen):
    stream = features_in
    rows = stream.shape[1]
    cols = stream.shape[2]
    side = rows * lax.axis_size("row")
    rounds = gain_outer.shape[0] // 4
    row_start = lax.axis_index("row") * rows
    col_start = lax.axis_index("col") * cols
    for repeat in range(rounds):
        stream = averaged_tiles(stream)
        for within in range(4):
            block = repeat * 4 + within
            dilation = 1 + within // 2
            outer_scale = gain_outer[block][:, None, None]
            outer_shift = bias_outer[block][:, None, None]
            inner_scale = gain_inner[block][:, None, None]
            inner_shift = bias_inner[block][:, None, None]
            deep = padded_2(stream, (("row", 1), ("col", 2)), 2 * dilation)
            hidden = jax.nn.relu(deep.astype(jnp.float32) * outer_scale + outer_shift)
            hidden = jnp.where(
                inside_mask(
                    row_start,
                    col_start,
                    2 * dilation,
                    rows + 4 * dilation,
                    cols + 4 * dilation,
                    side,
                ),
                hidden,
                0.0,
            ).astype(jnp.bfloat16)
            narrow = dilated_taps(
                hidden, w_narrow[block], dilation, rows + 2 * dilation, cols + 2 * dilation
            )
            inner = jax.nn.relu(narrow * inner_scale + inner_shift)
            inner = jnp.where(
                inside_mask(
                    row_start, col_start, dilation, rows + 2 * dilation, cols + 2 * dilation, side
                ),
                inner,
                0.0,
            ).astype(jnp.bfloat16)
            widened = dilated_taps(inner, w_widen[block], dilation, rows, cols)
            stream = (stream.astype(jnp.float32) + widened).astype(jnp.bfloat16)
    return stream


def solution(mesh):
    in_specs = (P(None, ("groups", "row"), "col"), P(), P(), P(), P(), P(), P())
    out_specs = P(None, ("groups", "row"), "col")
    return jax.shard_map(body, mesh=mesh, in_specs=in_specs, out_specs=out_specs, check_vma=False)
```

profile of v0, /device:TPU:8, one launch (start us, length us, event | category | flops | bytes accessed | tf_op | source)
XLA Modules:
  0.0 153.7 jit_solution(2823055591857940647)
XLA Ops:
  0.0 1.0 copy.37
  1.2 0.6 broadcast.270
  1.8 1.0 reduce.4
  2.8 0.7 reshape.335
  3.5 6.0 %all-to-all-start = ((bf16[32,2,512]{2,1,0:T(2,128)(2,1)}), bf16[32,2,512]{2,1,0:T(2,128)(2,1)S(1)}, u32[]{:S(2)}, u32[]{:S(2)}) async-start(bf16[32,2,512]{2,1,0:T(2,128)(2,1)} %reshape.335), calls=%async_computation | async-start | bytes 131072 | tf_op jit(solution)/shard_map/all_to_all | solution.py:48
  9.7 0.6 copy-done.3
  10.4 0.7 copy-done.5
  11.1 4.7 %all-to-all-done = bf16[32,2,512]{2,1,0:T(2,128)(2,1)S(1)} async-done(((bf16[32,2,512]{2,1,0:T(2,128)(2,1)}), bf16[32,2,512]{2,1,0:T(2,128)(2,1)S(1)}, u32[]{:S(2)}, u32[]{:S(2)}) %all-to-all-start) | async-done | bytes 65568 | tf_op jit(solution)/shard_map/all_to_all | solution.py:48
  15.8 0.3 convert_reduce_fusion.1
  16.6 0.7 copy-done.2
  17.3 1.9 %collective-permute-start = (bf16[64,2,128]{2,0,1:T(8,128)(2,1)S(1)}, bf16[64,2,128]{2,0,1:T(8,128)(2,1)S(1)}, u32[]{:S(2)}, u32[]{:S(2)}) collective-permute-start(bf16[64,2,128]{2,0,1:T(8,128)(2,1)S(1)} %get-tuple-element.43), channel_id=1, source_target_pairs={{0,1},{1,2},{2,3},{3,4},{4,5},{5,6},{6,7},{7,8},{8,9},{9,10},{10,1... | collective-permute-start | bytes 98312 | tf_op jit(solution)/shard_map/ppermute | solution.py:12
  19.2 5.4 %collective-permute-start.1 = (bf16[64,2,128]{2,0,1:T(8,128)(2,1)S(1)}, bf16[64,2,128]{2,0,1:T(8,128)(2,1)S(1)}, u32[]{:S(2)}, u32[]{:S(2)}) collective-permute-start(bf16[64,2,128]{2,0,1:T(8,128)(2,1)S(1)} %get-tuple-element.44), channel_id=1, source_target_pairs={{1,0},{2,1},{3,2},{4,3},{5,4},{6,5},{7,6},{8,7},{9,8},{10,9},{11,1... | collective-permute-start | bytes 98312 | tf_op jit(solution)/shard_map/ppermute | solution.py:15
  24.7 1.5 %collective-permute-done.1 = bf16[64,2,128]{2,0,1:T(8,128)(2,1)S(1)} collective-permute-done((bf16[64,2,128]{2,0,1:T(8,128)(2,1)S(1)}, bf16[64,2,128]{2,0,1:T(8,128)(2,1)S(1)}, u32[]{:S(2)}, u32[]{:S(2)}) %collective-permute-start.1) | collective-permute-done | bytes 32800 | tf_op jit(solution)/shard_map/ppermute | solution.py:15
  26.4 0.7 collective-permute-start.2
  27.1 0.7 collective-permute-start.3
  32.4 1.9 %collective-permute-start.4 = (bf16[64,2,128]{2,0,1:T(8,128)(2,1)S(1)}, bf16[64,2,128]{2,0,1:T(8,128)(2,1)S(1)}, u32[]{:S(2)}, u32[]{:S(2)}) collective-permute-start(bf16[64,2,128]{2,0,1:T(8,128)(2,1)S(1)} %get-tuple-element.41), channel_id=1, source_target_pairs={{0,1},{1,2},{2,3},{3,4},{4,5},{5,6},{6,7},{7,8},{8,9},{9,10},{10,1... | collective-permute-start | bytes 98312 | tf_op jit(solution)/shard_map/ppermute | solution.py:12
  34.3 5.4 %collective-permute-start.5 = (bf16[64,2,128]{2,0,1:T(8,128)(2,1)S(1)}, bf16[64,2,128]{2,0,1:T(8,128)(2,1)S(1)}, u32[]{:S(2)}, u32[]{:S(2)}) collective-permute-start(bf16[64,2,128]{2,0,1:T(8,128)(2,1)S(1)} %get-tuple-element.42), channel_id=1, source_target_pairs={{1,0},{2,1},{3,2},{4,3},{5,4},{6,5},{7,6},{8,7},{9,8},{10,9},{11,1... | collective-permute-start | bytes 98312 | tf_op jit(solution)/shard_map/ppermute | solution.py:15
  39.7 1.6 %collective-permute-done.5 = bf16[64,2,128]{2,0,1:T(8,128)(2,1)S(1)} collective-permute-done((bf16[64,2,128]{2,0,1:T(8,128)(2,1)S(1)}, bf16[64,2,128]{2,0,1:T(8,128)(2,1)S(1)}, u32[]{:S(2)}, u32[]{:S(2)}) %collective-permute-start.5) | collective-permute-done | bytes 32800 | tf_op jit(solution)/shard_map/ppermute | solution.py:15
  41.5 0.7 collective-permute-start.6
  42.1 0.7 collective-permute-start.7
  47.3 1.9 %collective-permute-start.8 = (bf16[64,4,128]{2,0,1:T(8,128)(2,1)S(1)}, bf16[64,4,128]{2,0,1:T(8,128)(2,1)S(1)}, u32[]{:S(2)}, u32[]{:S(2)}) collective-permute-start(bf16[64,4,128]{2,0,1:T(8,128)(2,1)S(1)} %fusion.65), channel_id=1, source_target_pairs={{0,1},{1,2},{2,3},{3,4},{4,5},{5,6},{6,7},{7,8},{8,9},{9,10},{10,1... | collective-permute-start | bytes 196616 | tf_op jit(solution)/shard_map/ppermute | solution.py:12
  49.2 5.5 %collective-permute-start.9 = (bf16[64,4,128]{2,0,1:T(8,128)(2,1)S(1)}, bf16[64,4,128]{2,0,1:T(8,128)(2,1)S(1)}, u32[]{:S(2)}, u32[]{:S(2)}) collective-permute-start(bf16[64,4,128]{2,0,1:T(8,128)(2,1)S(1)} %fusion.65), channel_id=1, source_target_pairs={{1,0},{2,1},{3,2},{4,3},{5,4},{6,5},{7,6},{8,7},{9,8},{10,9},{11,1... | collective-permute-start | bytes 196616 | tf_op jit(solution)/shard_map/ppermute | solution.py:15
  54.7 1.9 %collective-permute-done.9 = bf16[64,4,128]{2,0,1:T(8,128)(2,1)S(1)} collective-permute-done((bf16[64,4,128]{2,0,1:T(8,128)(2,1)S(1)}, bf16[64,4,128]{2,0,1:T(8,128)(2,1)S(1)}, u32[]{:S(2)}, u32[]{:S(2)}) %collective-permute-start.9) | collective-permute-done | bytes 65568 | tf_op jit(solution)/shard_map/ppermute | solution.py:15
  56.7 0.7 collective-permute-start.10
  57.4 0.7 collective-permute-start.11
  58.3 0.3 select_convert_fusion.3
  59.1 0.3 convolution_add_fusion.30
  60.7 0.3 fusion.40
  63.0 1.9 %collective-permute-start.12 = (bf16[64,4,128]{2,0,1:T(8,128)(2,1)S(1)}, bf16[64,4,128]{2,0,1:T(8,128)(2,1)S(1)}, u32[]{:S(2)}, u32[]{:S(2)}) collective-permute-start(bf16[64,4,128]{2,0,1:T(8,128)(2,1)S(1)} %fusion.66), channel_id=1, source_target_pairs={{0,1},{1,2},{2,3},{3,4},{4,5},{5,6},{6,7},{7,8},{8,9},{9,10},{10,1... | collective-permute-start | bytes 196616 | tf_op jit(solution)/shard_map/ppermute | solution.py:12
  64.9 5.5 %collective-permute-start.13 = (bf16[64,4,128]{2,0,1:T(8,128)(2,1)S(1)}, bf16[64,4,128]{2,0,1:T(8,128)(2,1)S(1)}, u32[]{:S(2)}, u32[]{:S(2)}) collective-permute-start(bf16[64,4,128]{2,0,1:T(8,128)(2,1)S(1)} %fusion.66), channel_id=1, source_target_pairs={{1,0},{2,1},{3,2},{4,3},{5,4},{6,5},{7,6},{8,7},{9,8},{10,9},{11,1... | collective-permute-start | bytes 196616 | tf_op jit(solution)/shard_map/ppermute | solution.py:15
  70.4 1.9 %collective-permute-done.13 = bf16[64,4,128]{2,0,1:T(8,128)(2,1)S(1)} collective-permute-done((bf16[64,4,128]{2,0,1:T(8,128)(2,1)S(1)}, bf16[64,4,128]{2,0,1:T(8,128)(2,1)S(1)}, u32[]{:S(2)}, u32[]{:S(2)}) %collective-permute-start.13) | collective-permute-done | bytes 65568 | tf_op jit(solution)/shard_map/ppermute | solution.py:15
  72.5 0.7 collective-permute-start.14
  73.1 0.8 collective-permute-start.15
  74.1 0.3 select_convert_fusion.2
  75.4 0.3 convolution_add_fusion.20
  76.5 0.3 fusion.41
  79.2 1.0 reduce.5
  80.2 10.6 %all_to_all.10 = bf16[32,2,512]{2,1,0:T(2,128)(2,1)S(1)} all-to-all(bf16[32,2,512]{2,1,0:T(2,128)(2,1)S(1)} %reshape.337), channel_id=1, replica_groups=mesh['groups'=1,'row'=32,'col'=1] {'row'}, dimensions={0} | all-to-all | bytes 131072 | tf_op jit(solution)/shard_map/all_to_all | solution.py:48
  90.9 0.3 convert_reduce_fusion
  91.7 1.9 %collective-permute-start.16 = (bf16[64,2,128]{2,0,1:T(8,128)(2,1)S(1)}, bf16[64,2,128]{2,0,1:T(8,128)(2,1)S(1)}, u32[]{:S(2)}, u32[]{:S(2)}) collective-permute-start(bf16[64,2,128]{2,0,1:T(8,128)(2,1)S(1)} %get-tuple-element.39), channel_id=1, source_target_pairs={{0,1},{1,2},{2,3},{3,4},{4,5},{5,6},{6,7},{7,8},{8,9},{9,10},{10,1... | collective-permute-start | bytes 98312 | tf_op jit(solution)/shard_map/ppermute | solution.py:12
  93.6 5.4 %collective-permute-start.17 = (bf16[64,2,128]{2,0,1:T(8,128)(2,1)S(1)}, bf16[64,2,128]{2,0,1:T(8,128)(2,1)S(1)}, u32[]{:S(2)}, u32[]{:S(2)}) collective-permute-start(bf16[64,2,128]{2,0,1:T(8,128)(2,1)S(1)} %get-tuple-element.40), channel_id=1, source_target_pairs={{1,0},{2,1},{3,2},{4,3},{5,4},{6,5},{7,6},{8,7},{9,8},{10,9},{11,1... | collective-permute-start | bytes 98312 | tf_op jit(solution)/shard_map/ppermute | solution.py:15
  99.1 1.6 %collective-permute-done.17 = bf16[64,2,128]{2,0,1:T(8,128)(2,1)S(1)} collective-permute-done((bf16[64,2,128]{2,0,1:T(8,128)(2,1)S(1)}, bf16[64,2,128]{2,0,1:T(8,128)(2,1)S(1)}, u32[]{:S(2)}, u32[]{:S(2)}) %collective-permute-start.17) | collective-permute-done | bytes 32800 | tf_op jit(solution)/shard_map/ppermute | solution.py:15
  100.8 0.7 collective-permute-start.18
  101.4 0.7 collective-permute-start.19
  106.6 1.9 %collective-permute-start.20 = (bf16[64,2,128]{2,0,1:T(8,128)(2,1)S(1)}, bf16[64,2,128]{2,0,1:T(8,128)(2,1)S(1)}, u32[]{:S(2)}, u32[]{:S(2)}) collective-permute-start(bf16[64,2,128]{2,0,1:T(8,128)(2,1)S(1)} %get-tuple-element.37), channel_id=1, source_target_pairs={{0,1},{1,2},{2,3},{3,4},{4,5},{5,6},{6,7},{7,8},{8,9},{9,10},{10,1... | collective-permute-start | bytes 98312 | tf_op jit(solution)/shard_map/ppermute | solution.py:12
  108.6 5.4 %collective-permute-start.21 = (bf16[64,2,128]{2,0,1:T(8,128)(2,1)S(1)}, bf16[64,2,128]{2,0,1:T(8,128)(2,1)S(1)}, u32[]{:S(2)}, u32[]{:S(2)}) collective-permute-start(bf16[64,2,128]{2,0,1:T(8,128)(2,1)S(1)} %get-tuple-element.38), channel_id=1, source_target_pairs={{1,0},{2,1},{3,2},{4,3},{5,4},{6,5},{7,6},{8,7},{9,8},{10,9},{11,1... | collective-permute-start | bytes 98312 | tf_op jit(solution)/shard_map/ppermute | solution.py:15
  114.0 1.6 %collective-permute-done.21 = bf16[64,2,128]{2,0,1:T(8,128)(2,1)S(1)} collective-permute-done((bf16[64,2,128]{2,0,1:T(8,128)(2,1)S(1)}, bf16[64,2,128]{2,0,1:T(8,128)(2,1)S(1)}, u32[]{:S(2)}, u32[]{:S(2)}) %collective-permute-start.21) | collective-permute-done | bytes 32800 | tf_op jit(solution)/shard_map/ppermute | solution.py:15
  115.7 0.7 collective-permute-start.22
  116.4 0.7 collective-permute-start.23
  121.6 1.9 %collective-permute-start.24 = (bf16[64,4,128]{2,0,1:T(8,128)(2,1)S(1)}, bf16[64,4,128]{2,0,1:T(8,128)(2,1)S(1)}, u32[]{:S(2)}, u32[]{:S(2)}) collective-permute-start(bf16[64,4,128]{2,0,1:T(8,128)(2,1)S(1)} %fusion.69), channel_id=1, source_target_pairs={{0,1},{1,2},{2,3},{3,4},{4,5},{5,6},{6,7},{7,8},{8,9},{9,10},{10,1... | collective-permute-start | bytes 196616 | tf_op jit(solution)/shard_map/ppermute | solution.py:12
  123.5 5.4 %collective-permute-start.25 = (bf16[64,4,128]{2,0,1:T(8,128)(2,1)S(1)}, bf16[64,4,128]{2,0,1:T(8,128)(2,1)S(1)}, u32[]{:S(2)}, u32[]{:S(2)}) collective-permute-start(bf16[64,4,128]{2,0,1:T(8,128)(2,1)S(1)} %fusion.69), channel_id=1, source_target_pairs={{1,0},{2,1},{3,2},{4,3},{5,4},{6,5},{7,6},{8,7},{9,8},{10,9},{11,1... | collective-permute-start | bytes 196616 | tf_op jit(solution)/shard_map/ppermute | solution.py:15
  129.0 1.9 %collective-permute-done.25 = bf16[64,4,128]{2,0,1:T(8,128)(2,1)S(1)} collective-permute-done((bf16[64,4,128]{2,0,1:T(8,128)(2,1)S(1)}, bf16[64,4,128]{2,0,1:T(8,128)(2,1)S(1)}, u32[]{:S(2)}, u32[]{:S(2)}) %collective-permute-start.25) | collective-permute-done | bytes 65568 | tf_op jit(solution)/shard_map/ppermute | solution.py:15
  131.0 0.7 collective-permute-start.26
  131.7 0.7 collective-permute-start.27
  132.5 0.3 select_convert_fusion.1
  134.8 0.3 fusion.42
  137.2 1.9 %collective-permute-start.28 = (bf16[64,4,128]{2,0,1:T(8,128)(2,1)S(1)}, bf16[64,4,128]{2,0,1:T(8,128)(2,1)S(1)}, u32[]{:S(2)}, u32[]{:S(2)}) collective-permute-start(bf16[64,4,128]{2,0,1:T(8,128)(2,1)S(1)} %fusion.70), channel_id=1, source_target_pairs={{0,1},{1,2},{2,3},{3,4},{4,5},{5,6},{6,7},{7,8},{8,9},{9,10},{10,1... | collective-permute-start | bytes 196616 | tf_op jit(solution)/shard_map/ppermute | solution.py:12
  139.1 5.5 %collective-permute-start.29 = (bf16[64,4,128]{2,0,1:T(8,128)(2,1)S(1)}, bf16[64,4,128]{2,0,1:T(8,128)(2,1)S(1)}, u32[]{:S(2)}, u32[]{:S(2)}) collective-permute-start(bf16[64,4,128]{2,0,1:T(8,128)(2,1)S(1)} %fusion.70), channel_id=1, source_target_pairs={{1,0},{2,1},{3,2},{4,3},{5,4},{6,5},{7,6},{8,7},{9,8},{10,9},{11,1... | collective-permute-start | bytes 196616 | tf_op jit(solution)/shard_map/ppermute | solution.py:15
  144.6 1.9 %collective-permute-done.29 = bf16[64,4,128]{2,0,1:T(8,128)(2,1)S(1)} collective-permute-done((bf16[64,4,128]{2,0,1:T(8,128)(2,1)S(1)}, bf16[64,4,128]{2,0,1:T(8,128)(2,1)S(1)}, u32[]{:S(2)}, u32[]{:S(2)}) %collective-permute-start.29) | collective-permute-done | bytes 65568 | tf_op jit(solution)/shard_map/ppermute | solution.py:15
  146.6 0.7 collective-permute-start.30
  147.3 0.9 collective-permute-start.31
  148.3 0.3 select_convert_fusion
  150.7 0.3 fusion.43
  153.0 0.7 copy.55
  (234 shorter events, 36.6 us)
Async XLA Ops:
  1.1 8.5 %copy-start.1 = (bf16[8,32,576]{2,1,0:T(8,128)(2,1)S(1)}, bf16[8,32,576]{2,1,0:T(8,128)(2,1)}, u32[]{:S(2)}) copy-start(bf16[8,32,576]{2,1,0:T(8,128)(2,1)} %param.10) | copy-start | bytes 884740
  3.5 6.1 %copy-start = (bf16[8,64,288]{2,1,0:T(8,128)(2,1)S(1)}, bf16[8,64,288]{2,1,0:T(8,128)(2,1)}, u32[]{:S(2)}) copy-start(bf16[8,64,288]{2,1,0:T(8,128)(2,1)} %param.13) | copy-start | bytes 884740
  3.5 12.3 %all-to-all-start = ((bf16[32,2,512]{2,1,0:T(2,128)(2,1)}), bf16[32,2,512]{2,1,0:T(2,128)(2,1)S(1)}, u32[]{:S(2)}, u32[]{:S(2)}) async-start(bf16[32,2,512]{2,1,0:T(2,128)(2,1)} %reshape.335), calls=%async_computation | async-start | bytes 131072 | tf_op jit(solution)/shard_map/all_to_all | solution.py:48
  9.6 0.7 copy-start.3
  9.7 0.7 copy-start.4
  10.3 0.7 copy-start.5
  10.3 0.7 copy-start.6
  16.4 0.8 copy-start.2
  17.3 7.4 %collective-permute-start = (bf16[64,2,128]{2,0,1:T(8,128)(2,1)S(1)}, bf16[64,2,128]{2,0,1:T(8,128)(2,1)S(1)}, u32[]{:S(2)}, u32[]{:S(2)}) collective-permute-start(bf16[64,2,128]{2,0,1:T(8,128)(2,1)S(1)} %get-tuple-element.43), channel_id=1, source_target_pairs={{0,1},{1,2},{2,3},{3,4},{4,5},{5,6},{6,7},{7,8},{8,9},{9,10},{10,1... | collective-permute-start | bytes 98312 | tf_op jit(solution)/shard_map/ppermute | solution.py:12
  19.2 7.0 %collective-permute-start.1 = (bf16[64,2,128]{2,0,1:T(8,128)(2,1)S(1)}, bf16[64,2,128]{2,0,1:T(8,128)(2,1)S(1)}, u32[]{:S(2)}, u32[]{:S(2)}) collective-permute-start(bf16[64,2,128]{2,0,1:T(8,128)(2,1)S(1)} %get-tuple-element.44), channel_id=1, source_target_pairs={{1,0},{2,1},{3,2},{4,3},{5,4},{6,5},{7,6},{8,7},{9,8},{10,9},{11,1... | collective-permute-start | bytes 98312 | tf_op jit(solution)/shard_map/ppermute | solution.py:15
  26.4 1.5 %collective-permute-start.2 = (bf16[64,8,2]{2,0,1:T(8,128)(2,1)S(1)}, bf16[64,8,2]{2,0,1:T(8,128)(2,1)S(1)}, u32[]{:S(2)}, u32[]{:S(2)}) collective-permute-start(bf16[64,8,2]{2,0,1:T(8,128)(2,1)S(1)} %get-tuple-element.35), channel_id=1, source_target_pairs={} | collective-permute-start | bytes 6152 | tf_op jit(solution)/shard_map/ppermute | solution.py:12
  27.1 0.9 collective-permute-start.3
  32.4 7.4 %collective-permute-start.4 = (bf16[64,2,128]{2,0,1:T(8,128)(2,1)S(1)}, bf16[64,2,128]{2,0,1:T(8,128)(2,1)S(1)}, u32[]{:S(2)}, u32[]{:S(2)}) collective-permute-start(bf16[64,2,128]{2,0,1:T(8,128)(2,1)S(1)} %get-tuple-element.41), channel_id=1, source_target_pairs={{0,1},{1,2},{2,3},{3,4},{4,5},{5,6},{6,7},{7,8},{8,9},{9,10},{10,1... | collective-permute-start | bytes 98312 | tf_op jit(solution)/shard_map/ppermute | solution.py:12
  34.3 7.0 %collective-permute-start.5 = (bf16[64,2,128]{2,0,1:T(8,128)(2,1)S(1)}, bf16[64,2,128]{2,0,1:T(8,128)(2,1)S(1)}, u32[]{:S(2)}, u32[]{:S(2)}) collective-permute-start(bf16[64,2,128]{2,0,1:T(8,128)(2,1)S(1)} %get-tuple-element.42), channel_id=1, source_target_pairs={{1,0},{2,1},{3,2},{4,3},{5,4},{6,5},{7,6},{8,7},{9,8},{10,9},{11,1... | collective-permute-start | bytes 98312 | tf_op jit(solution)/shard_map/ppermute | solution.py:15
  41.5 1.5 collective-permute-start.6
  42.1 0.8 collective-permute-start.7
  47.3 7.4 %collective-permute-start.8 = (bf16[64,4,128]{2,0,1:T(8,128)(2,1)S(1)}, bf16[64,4,128]{2,0,1:T(8,128)(2,1)S(1)}, u32[]{:S(2)}, u32[]{:S(2)}) collective-permute-start(bf16[64,4,128]{2,0,1:T(8,128)(2,1)S(1)} %fusion.65), channel_id=1, source_target_pairs={{0,1},{1,2},{2,3},{3,4},{4,5},{5,6},{6,7},{7,8},{8,9},{9,10},{10,1... | collective-permute-start | bytes 196616 | tf_op jit(solution)/shard_map/ppermute | solution.py:12
  49.2 7.3 %collective-permute-start.9 = (bf16[64,4,128]{2,0,1:T(8,128)(2,1)S(1)}, bf16[64,4,128]{2,0,1:T(8,128)(2,1)S(1)}, u32[]{:S(2)}, u32[]{:S(2)}) collective-permute-start(bf16[64,4,128]{2,0,1:T(8,128)(2,1)S(1)} %fusion.65), channel_id=1, source_target_pairs={{1,0},{2,1},{3,2},{4,3},{5,4},{6,5},{7,6},{8,7},{9,8},{10,9},{11,1... | collective-permute-start | bytes 196616 | tf_op jit(solution)/shard_map/ppermute | solution.py:15
  56.7 1.5 %collective-permute-start.10 = (bf16[64,12,4]{2,0,1:T(8,128)(2,1)S(1)}, bf16[64,12,4]{2,0,1:T(8,128)(2,1)S(1)}, u32[]{:S(2)}, u32[]{:S(2)}) collective-permute-start(bf16[64,12,4]{2,0,1:T(8,128)(2,1)S(1)} %get-tuple-element.27), channel_id=1, source_target_pairs={} | collective-permute-start | bytes 18440 | tf_op jit(solution)/shard_map/ppermute | solution.py:12
  57.4 0.9 collective-permute-start.11
  63.0 7.4 %collective-permute-start.12 = (bf16[64,4,128]{2,0,1:T(8,128)(2,1)S(1)}, bf16[64,4,128]{2,0,1:T(8,128)(2,1)S(1)}, u32[]{:S(2)}, u32[]{:S(2)}) collective-permute-start(bf16[64,4,128]{2,0,1:T(8,128)(2,1)S(1)} %fusion.66), channel_id=1, source_target_pairs={{0,1},{1,2},{2,3},{3,4},{4,5},{5,6},{6,7},{7,8},{8,9},{9,10},{10,1... | collective-permute-start | bytes 196616 | tf_op jit(solution)/shard_map/ppermute | solution.py:12
  64.9 7.4 %collective-permute-start.13 = (bf16[64,4,128]{2,0,1:T(8,128)(2,1)S(1)}, bf16[64,4,128]{2,0,1:T(8,128)(2,1)S(1)}, u32[]{:S(2)}, u32[]{:S(2)}) collective-permute-start(bf16[64,4,128]{2,0,1:T(8,128)(2,1)S(1)} %fusion.66), channel_id=1, source_target_pairs={{1,0},{2,1},{3,2},{4,3},{5,4},{6,5},{7,6},{8,7},{9,8},{10,9},{11,1... | collective-permute-start | bytes 196616 | tf_op jit(solution)/shard_map/ppermute | solution.py:15
  72.5 1.7 %collective-permute-start.14 = (bf16[64,12,4]{2,0,1:T(8,128)(2,1)S(1)}, bf16[64,12,4]{2,0,1:T(8,128)(2,1)S(1)}, u32[]{:S(2)}, u32[]{:S(2)}) collective-permute-start(bf16[64,12,4]{2,0,1:T(8,128)(2,1)S(1)} %get-tuple-element.25), channel_id=1, source_target_pairs={} | collective-permute-start | bytes 18440 | tf_op jit(solution)/shard_map/ppermute | solution.py:12
  73.1 1.0 collective-permute-start.15
  91.7 7.4 %collective-permute-start.16 = (bf16[64,2,128]{2,0,1:T(8,128)(2,1)S(1)}, bf16[64,2,128]{2,0,1:T(8,128)(2,1)S(1)}, u32[]{:S(2)}, u32[]{:S(2)}) collective-permute-start(bf16[64,2,128]{2,0,1:T(8,128)(2,1)S(1)} %get-tuple-element.39), channel_id=1, source_target_pairs={{0,1},{1,2},{2,3},{3,4},{4,5},{5,6},{6,7},{7,8},{8,9},{9,10},{10,1... | collective-permute-start | bytes 98312 | tf_op jit(solution)/shard_map/ppermute | solution.py:12
  93.6 7.0 %collective-permute-start.17 = (bf16[64,2,128]{2,0,1:T(8,128)(2,1)S(1)}, bf16[64,2,128]{2,0,1:T(8,128)(2,1)S(1)}, u32[]{:S(2)}, u32[]{:S(2)}) collective-permute-start(bf16[64,2,128]{2,0,1:T(8,128)(2,1)S(1)} %get-tuple-element.40), channel_id=1, source_target_pairs={{1,0},{2,1},{3,2},{4,3},{5,4},{6,5},{7,6},{8,7},{9,8},{10,9},{11,1... | collective-permute-start | bytes 98312 | tf_op jit(solution)/shard_map/ppermute | solution.py:15
  100.8 1.5 collective-permute-start.18
  101.4 0.8 collective-permute-start.19
  106.6 7.4 %collective-permute-start.20 = (bf16[64,2,128]{2,0,1:T(8,128)(2,1)S(1)}, bf16[64,2,128]{2,0,1:T(8,128)(2,1)S(1)}, u32[]{:S(2)}, u32[]{:S(2)}) collective-permute-start(bf16[64,2,128]{2,0,1:T(8,128)(2,1)S(1)} %get-tuple-element.37), channel_id=1, source_target_pairs={{0,1},{1,2},{2,3},{3,4},{4,5},{5,6},{6,7},{7,8},{8,9},{9,10},{10,1... | collective-permute-start | bytes 98312 | tf_op jit(solution)/shard_map/ppermute | solution.py:12
  108.6 7.0 %collective-permute-start.21 = (bf16[64,2,128]{2,0,1:T(8,128)(2,1)S(1)}, bf16[64,2,128]{2,0,1:T(8,128)(2,1)S(1)}, u32[]{:S(2)}, u32[]{:S(2)}) collective-permute-start(bf16[64,2,128]{2,0,1:T(8,128)(2,1)S(1)} %get-tuple-element.38), channel_id=1, source_target_pairs={{1,0},{2,1},{3,2},{4,3},{5,4},{6,5},{7,6},{8,7},{9,8},{10,9},{11,1... | collective-permute-start | bytes 98312 | tf_op jit(solution)/shard_map/ppermute | solution.py:15
  115.7 1.5 collective-permute-start.22
  116.4 0.8 collective-permute-start.23
  121.6 7.4 %collective-permute-start.24 = (bf16[64,4,128]{2,0,1:T(8,128)(2,1)S(1)}, bf16[64,4,128]{2,0,1:T(8,128)(2,1)S(1)}, u32[]{:S(2)}, u32[]{:S(2)}) collective-permute-start(bf16[64,4,128]{2,0,1:T(8,128)(2,1)S(1)} %fusion.69), channel_id=1, source_target_pairs={{0,1},{1,2},{2,3},{3,4},{4,5},{5,6},{6,7},{7,8},{8,9},{9,10},{10,1... | collective-permute-start | bytes 196616 | tf_op jit(solution)/shard_map/ppermute | solution.py:12
  123.5 7.3 %collective-permute-start.25 = (bf16[64,4,128]{2,0,1:T(8,128)(2,1)S(1)}, bf16[64,4,128]{2,0,1:T(8,128)(2,1)S(1)}, u32[]{:S(2)}, u32[]{:S(2)}) collective-permute-start(bf16[64,4,128]{2,0,1:T(8,128)(2,1)S(1)} %fusion.69), channel_id=1, source_target_pairs={{1,0},{2,1},{3,2},{4,3},{5,4},{6,5},{7,6},{8,7},{9,8},{10,9},{11,1... | collective-permute-start | bytes 196616 | tf_op jit(solution)/shard_map/ppermute | solution.py:15
  131.0 1.5 collective-permute-start.26
  131.7 0.8 collective-permute-start.27
  137.2 7.4 %collective-permute-start.28 = (bf16[64,4,128]{2,0,1:T(8,128)(2,1)S(1)}, bf16[64,4,128]{2,0,1:T(8,128)(2,1)S(1)}, u32[]{:S(2)}, u32[]{:S(2)}) collective-permute-start(bf16[64,4,128]{2,0,1:T(8,128)(2,1)S(1)} %fusion.70), channel_id=1, source_target_pairs={{0,1},{1,2},{2,3},{3,4},{4,5},{5,6},{6,7},{7,8},{8,9},{9,10},{10,1... | collective-permute-start | bytes 196616 | tf_op jit(solution)/shard_map/ppermute | solution.py:12
  139.1 7.4 %collective-permute-start.29 = (bf16[64,4,128]{2,0,1:T(8,128)(2,1)S(1)}, bf16[64,4,128]{2,0,1:T(8,128)(2,1)S(1)}, u32[]{:S(2)}, u32[]{:S(2)}) collective-permute-start(bf16[64,4,128]{2,0,1:T(8,128)(2,1)S(1)} %fusion.70), channel_id=1, source_target_pairs={{1,0},{2,1},{3,2},{4,3},{5,4},{6,5},{7,6},{8,7},{9,8},{10,9},{11,1... | collective-permute-start | bytes 196616 | tf_op jit(solution)/shard_map/ppermute | solution.py:15
  146.6 1.7 %collective-permute-start.30 = (bf16[64,12,4]{2,0,1:T(8,128)(2,1)S(1)}, bf16[64,12,4]{2,0,1:T(8,128)(2,1)S(1)}, u32[]{:S(2)}, u32[]{:S(2)}) collective-permute-start(bf16[64,12,4]{2,0,1:T(8,128)(2,1)S(1)} %get-tuple-element.21), channel_id=1, source_target_pairs={} | collective-permute-start | bytes 18440 | tf_op jit(solution)/shard_map/ppermute | solution.py:12
  147.3 1.0 collective-permute-start.31
where the time goes:
time: 156 us; the launch traced here: 154 us
  starting transfers between devices  76.1 us (49%)
  matrix products  33.4 us (21%)
  waiting for transfers between devices  18.4 us (12%)
  blocking collectives  10.6 us (7%)
  local copies, waits for them, and re-layouts  8.35 us (5%)
  other arithmetic  5.54 us (4%)
    ppermute x16, starting transfers between devices, padded_2(): lax.ppermute(lax.slice_in_dim(block, 0, width, axis=dim), axis, backward)  49.4 us
    dot_general x144, matrix products, dilated_taps(): jnp.einsum('oc,crw->orw', weight_tap, window, preferred_element_type=jnp....  33.4 us
    ppermute x16, starting transfers between devices, padded_2(): lax.ppermute(lax.slice_in_dim(block, block.shape[dim] - width, None, axis...  20.7 us
    ppermute x16, waiting for transfers between devices, padded_2(): lax.ppermute(lax.slice_in_dim(block, 0, width, axis=dim), axis, backward)  13.7 us
    all_to_all x1, blocking collectives, mirrored(): lax.all_to_all(outgoing, 'row', split_axis=1, concat_axis=1, tiled=True)  10.6 us
    all_to_all x1, starting transfers between devices, mirrored(): lax.all_to_all(outgoing, 'row', split_axis=1, concat_axis=1, tiled=True)  6.04 us
    unnamed x28, local copies, waits for them, and re-layouts  5.39 us
    all_to_all x1, waiting for transfers between devices, mirrored(): lax.all_to_all(outgoing, 'row', split_axis=1, concat_axis=1, tiled=True)  4.65 us
  transfers between devices with their start and end apart: 33, of which 9 were waited for; matrix products, arithmetic and copies ran while one was open for 1% of the time, Pallas kernels for 0%

commit v1 on v0

--- a/solution.py
+++ b/solution.py
@@ -1,7 +1,324 @@
+import functools
+
+import numpy as np
 import jax
 import jax.numpy as jnp
 from jax import lax
+from jax.experimental import pallas as pl
+from jax.experimental.pallas import tpu as pltpu
 from jax.sharding import PartitionSpec as P
+
+GROUPS = ((1, 1), (2, 2))
+LANES = 128
+
+
+def remote(src, dst, send_sem, recv_sem, target):
+    return pltpu.make_async_remote_copy(
+        src_ref=src,
+        dst_ref=dst,
+        send_sem=send_sem,
+        recv_sem=recv_sem,
+        device_id={"row": target},
+        device_id_type=pl.DeviceIdType.MESH,
+    )
+
+
+def spread_constants(rows, channels, width):
+    count = width // rows
+    halves = rows * channels // LANES
+    pieces = rows * halves
+    subs = LANES // channels
+    p = np.arange(width * halves)
+    pack = np.zeros((width * halves, halves * width), np.float32)
+    pack[p, (p % halves) * width + p // halves] = 1
+    o = np.arange(rows * width)
+    xx, x = o // width, o % width
+    j, r = x // rows, x % rows
+    q = (r % subs) * (count * pieces) + j * pieces + xx * halves + r // subs
+    unpack = np.zeros((subs * count * pieces, rows * width), np.float32)
+    unpack[q, o] = 1
+    return jnp.asarray(pack, jnp.bfloat16), jnp.asarray(unpack, jnp.bfloat16)
+
+
+def shifted_sum(parts, dilation, lane):
+    width = lane.shape[-1]
+    low = jnp.where(lane < dilation, 0.0, pltpu.roll(parts[0], dilation, 1))
+    high = jnp.where(lane >= width - dilation, 0.0, pltpu.roll(parts[2], width - dilation, 1))
+    return parts[1] + low + high
+
+
+def network_kernel(
+    count, rounds, x_ref, params_ref, wn_ref, ww_ref, pack_ref, unpack_ref, out_ref, *scratch
+):
+    rows, channels, width = x_ref.shape
+    mid = ww_ref.shape[2] // 3
+    side = rows * count
+    halves = rows * channels // LANES
+    subs = LANES // channels
+    pieces = rows * halves
+    groups = len(GROUPS)
+    tiles = scratch[: rounds * groups]
+    sent, got, stream_buf, hidden_buf, inner_buf = scratch[rounds * groups : rounds * groups + 5]
+    mirror_send, mirror_recv, halo_send, halo_recv = scratch[rounds * groups + 5 :]
+    me = lax.axis_index("row")
+
+    barrier = pltpu.get_barrier_semaphore()
+
+    def greet(k, carry):
+        pl.semaphore_signal(
+            barrier,
+            inc=1,
+            device_id={"row": lax.rem(me + k, count)},
+            device_id_type=pl.DeviceIdType.MESH,
+        )
+        return carry
+
+    lax.fori_loop(1, count, greet, 0)
+    for phase in range(rounds * groups):
+        tile = tiles[phase]
+        reach = tile.shape[0] // 2
+        for k in range(1, reach + 1):
+            for sign in (-1, 1):
+                slot = reach + sign * k
+                other = me + sign * k
+
+                @pl.when((other < 0) | (other >= count))
+                def _():
+                    tile[slot] = jnp.zeros(tile.shape[1:], tile.dtype)
+
+    def pack(rd, stream):
+        flat = [s for s in stream]
+        per = LANES // channels
+        cat = jnp.concatenate(
+            [jnp.concatenate(flat[h * per : (h + 1) * per], axis=0) for h in range(halves)], axis=1
+        )
+        packed = lax.dot_general(
+            pack_ref[...], cat, (((1,), (1,)), ((), ())), preferred_element_type=jnp.float32
+        )
+        sent[rd] = packed.reshape(count, pieces, LANES).astype(jnp.bfloat16)
+
+    def mirror_copy(rd, target, source):
+        return remote(
+            sent.at[rd, target],
+            got.at[rd, source],
+            mirror_send.at[rd, target],
+            mirror_recv.at[rd, source],
+            target,
+        )
+
+    lane = lax.broadcasted_iota(jnp.int32, (1, width), 1)
+    stream = [x_ref[r] for r in range(rows)]
+    pack(0, stream)
+    pl.semaphore_wait(barrier, count - 1)
+
+    for rd in range(rounds):
+        if rd:
+            pack(rd, stream)
+
+        def send(k, carry):
+            mirror_copy(rd, lax.rem(me + k, count), me).start()
+            return carry
+
+        def receive(k, carry):
+            source = lax.rem(me + k, count)
+            mirror_copy(rd, source, source).wait_recv()
+            return carry
+
+        lax.fori_loop(1, count, send, 0)
+        got[rd, me] = sent[rd, me]
+        lax.fori_loop(1, count, receive, 0)
+
+        arrived = got[rd].astype(jnp.float32).reshape(count * pieces, LANES).T
+        arrived = jnp.concatenate(
+            [arrived[u * channels : (u + 1) * channels] for u in range(subs)], axis=1
+        ).astype(jnp.bfloat16)
+        partner = jnp.dot(arrived, unpack_ref[...], preferred_element_type=jnp.float32)
+        stream = [
+            (
+                (stream[r].astype(jnp.float32) + partner[:, r * width : (r + 1) * width]) * 0.5
+            ).astype(jnp.bfloat16)
+            for r in range(rows)
+        ]
+
+        block = rd * sum(len(g) for g in GROUPS)
+        for gi, group in enumerate(GROUPS):
+            phase = rd * groups + gi
+            tile = tiles[phase]
+            reach = tile.shape[0] // 2
+            for r in range(rows):
+                tile[reach, r] = stream[r]
+
+            def halo_copy(k, slot_there, target):
+                return remote(
+                    tile.at[reach],
+                    tile.at[slot_there],
+                    halo_send.at[phase, reach + k],
+                    halo_recv.at[phase, slot_there],
+                    target,
+                )
+
+            offsets = [s * k for k in range(1, reach + 1) for s in (-1, 1)]
+            for k in offsets:
+
+                @pl.when((me + k >= 0) & (me + k < count))
+                def _():
+                    halo_copy(k, reach - k, me + k).start()
+
+            for k in offsets:
+
+                @pl.when((me + k >= 0) & (me + k < count))
+                def _():
+                    halo_copy(k, reach + k, me + k).wait_recv()
+
+            halo = 2 * sum(group)
+            lo = reach * rows - halo
+            hi = (reach + 1) * rows + halo
+            first_row = (me - reach) * rows
+
+            def inside(e):
+                g = first_row + e
+                return jnp.where((g >= 0) & (g < side), 1.0, 0.0).astype(jnp.float32)
+
+            def masked(value, e):
+                if reach * rows <= e < (reach + 1) * rows:
+                    return value
+                return value * inside(e)
+
+            for bi, d in enumerate(group):
+
+                def param(start, size):
+                    return jnp.broadcast_to(
+                        params_ref[start : start + size, block : block + 1], (size, width)
+                    )
+
+                scale_o = param(0, channels)
+                shift_o = param(channels, channels)
+                scale_i = param(2 * channels, mid)
+                shift_i = param(2 * channels + mid, mid)
+
+                def load(e):
+                    return tile[e // rows, e % rows] if bi == 0 else stream_buf[e]
+
+                for e in range(lo, hi):
+                    value = jnp.maximum(load(e).astype(jnp.float32) * scale_o + shift_o, 0.0)
+                    hidden_buf[e] = masked(value, e).astype(jnp.bfloat16)
+                for e in range(lo + d, hi - d, 2):
+                    both = jnp.concatenate(
+                        [
+                            jnp.concatenate([hidden_buf[e + i + (ky - 1) * d] for ky in range(3)], axis=0)
+                            for i in range(2)
+                        ],
+                        axis=1,
+                    )
+                    y = jnp.dot(wn_ref[block], both, preferred_element_type=jnp.float32)
+                    for i in range(2):
+                        parts = [
+                            y[kx * mid : (kx + 1) * mid, i * width : (i + 1) * width]
+                            for kx in range(3)
+                        ]
+                        narrow = shifted_sum(parts, d, lane)
+                        value = jnp.maximum(narrow * scale_i + shift_i, 0.0)
+                        inner_buf[e + i] = masked(value, e + i).astype(jnp.bfloat16)
+                lo, hi = lo + 2 * d, hi - 2 * d
+                final = bi == len(group) - 1
+                stream = [None] * rows
+                for e in range(lo, hi, 2):
+                    both = jnp.concatenate(
+                        [
+                            jnp.concatenate([inner_buf[e + i + (ky - 1) * d] for ky in range(3)], axis=0)
+                            for i in range(2)
+                        ],
+                        axis=1,
+                    )
+                    y = jnp.dot(ww_ref[block], both, preferred_element_type=jnp.float32)
+                    for i in range(2):
+                        parts = [
+                            y[kx * channels : (kx + 1) * channels, i * width : (i + 1) * width]
+                            for kx in range(3)
+                        ]
+                        widened = shifted_sum(parts, d, lane)
+                        value = (load(e + i).astype(jnp.float32) + widened).astype(jnp.bfloat16)
+                        if final:
+                            stream[e + i - lo] = value
+                        else:
+                            stream_buf[e + i] = value
+                block += 1
+
+    for r in range(rows):
+        out_ref[r] = stream[r]
+
+    for rd in range(rounds):
+
+        def finish(k, carry):
+            target = lax.rem(me + k, count)
+            mirror_copy(rd, target, me).wait_send()
+            return carry
+
+        lax.fori_loop(1, count, finish, 0)
+        for gi in range(groups):
+            phase = rd * groups + gi
+            tile = tiles[phase]
+            reach = tile.shape[0] // 2
+            for k in [s * k for k in range(1, reach + 1) for s in (-1, 1)]:
+
+                @pl.when((me + k >= 0) & (me + k < count))
+                def _():
+                    remote(
+                        tile.at[reach],
+                        tile.at[reach - k],
+                        halo_send.at[phase, reach + k],
+                        halo_recv.at[phase, reach - k],
+                        me + k,
+                    ).wait_send()
+
+
+def fused_body(features_in, gain_outer, bias_outer, w_narrow, gain_inner, bias_inner, w_widen):
+    channels, rows, width = features_in.shape
+    blocks, mid = gain_inner.shape
+    count = lax.axis_size("row")
+    rounds = blocks // sum(len(g) for g in GROUPS)
+    halves = rows * channels // LANES
+    pack, unpack = spread_constants(rows, channels, width)
+    params = jnp.concatenate([gain_outer, bias_outer, gain_inner, bias_inner], axis=1).T
+    wn = w_narrow.reshape(blocks, mid, 3, 3, channels).transpose(0, 3, 1, 2, 4)
+    ww = w_widen.reshape(blocks, channels, 3, 3, mid).transpose(0, 3, 1, 2, 4)
+    reaches = [-(-2 * sum(g) // rows) for g in GROUPS]
+    tall = (2 * max(reaches) + 1) * rows
+    phases = rounds * len(GROUPS)
+    dma = pltpu.SemaphoreType.DMA
+    out = pl.pallas_call(
+        functools.partial(network_kernel, count, rounds),
+        out_shape=jax.ShapeDtypeStruct((rows, channels, width), jnp.bfloat16),
+        in_specs=[pl.BlockSpec(memory_space=pltpu.VMEM)] * 6,
+        out_specs=pl.BlockSpec(memory_space=pltpu.VMEM),
+        scratch_shapes=[
+            pltpu.VMEM((2 * r + 1, rows, channels, width), jnp.bfloat16)
+            for _ in range(rounds)
+            for r in reaches
+        ]
+        + [
+            pltpu.VMEM((rounds, count, rows * halves, LANES), jnp.bfloat16),
+            pltpu.VMEM((rounds, count, rows * halves, LANES), jnp.bfloat16),
+            pltpu.VMEM((tall, channels, width), jnp.bfloat16),
+            pltpu.VMEM((tall, channels, width), jnp.bfloat16),
+            pltpu.VMEM((tall, mid, width), jnp.bfloat16),
+            dma((rounds, count)),
+            dma((rounds, count)),
+            dma((phases, 2 * max(reaches) + 1)),
+            dma((phases, 2 * max(reaches) + 1)),
+        ],
+        compiler_params=pltpu.CompilerParams(
+            collective_id=0, has_side_effects=True, vmem_limit_bytes=32 * 1024 * 1024
+        ),
+    )(
+        features_in.transpose(1, 0, 2),
+        params,
+        wn.reshape(blocks, 3 * mid, 3 * channels),
+        ww.reshape(blocks, 3 * channels, 3 * mid),
+        pack,
+        unpack,
+    )
+    return out.transpose(1, 0, 2)
 
 
 def padded_2(block, sides, width):
@@ -120,7 +437,23 @@
     return stream
 
 
+def dispatch(mesh, *args):
+    channels, rows, width = args[0].shape
+    whole_rows = mesh.shape["col"] == 1 and width == rows * mesh.shape["row"]
+    packs = LANES % channels == 0 and rows * channels % LANES == 0 and width % LANES == 0
+    even = rows % 2 == 0 and rows * rows * channels % (8 * LANES) == 0
+    if whole_rows and packs and even:
+        return fused_body(*args)
+    return body(*args)
+
+
 def solution(mesh):
     in_specs = (P(None, ("groups", "row"), "col"), P(), P(), P(), P(), P(), P())
     out_specs = P(None, ("groups", "row"), "col")
-    return jax.shard_map(body, mesh=mesh, in_specs=in_specs, out_specs=out_specs, check_vma=False)
+    return jax.shard_map(
+        functools.partial(dispatch, mesh),
+        mesh=mesh,
+        in_specs=in_specs,
+        out_specs=out_specs,
+        check_vma=False,
+    )

time: 156 us -> 49.2 us (0.32)
  the two profiles are of different devices: /device:TPU:8 before, /device:TPU:5 now
where the time goes in v1:
time: 49.2 us; the launch traced here: 48.9 us
  Pallas kernels  41.7 us (85%)
  local copies, waits for them, and re-layouts  7.06 us (14%)
    pallas_call x1, Pallas kernels, fused_body(): pl.pallas_call(functools.partial(network_kernel, count, rounds), out_shap...  41.7 us
    unnamed x16, local copies, waits for them, and re-layouts  2.59 us
    reshape x1, local copies, waits for them, and re-layouts, fused_body(): wn = w_narrow.reshape(blocks, mid, 3, 3, channels).transpose(0, 3, 1, 2, 4)  1.7 us

profile of v1, /device:TPU:5, one launch (start us, length us, event | category | flops | bytes accessed | tf_op | source)
XLA Modules:
  0.0 48.9 jit_solution(3801404935420719852)
XLA Ops:
  0.0 0.0 copy-start.3
  0.0 0.0 copy-start.4
  0.0 0.0 copy-start.5
  0.0 0.0 copy-start.6
  0.0 0.9 %copy.36 = bf16[64,4,128]{2,0,1:T(8,128)(2,1)S(1)} copy(bf16[64,4,128]{2,1,0:T(4,128)(2,1)} %param.9) | data formatting | bytes 131072 | tf_op args[0]
  0.9 0.0 copy-done.3
  0.9 0.0 copy-done.4
  0.9 0.0 copy-done.5
  0.9 0.0 copy-done.6
  1.0 0.1 pad_maximum_fusion
  1.0 0.1 copy.29
  1.1 1.7 %reshape.12 = bf16[8,32,3,3,64]{4,3,2,1,0:T(4,128)(2,1)S(1)} reshape(bf16[8,32,576]{2,1,0:T(8,128)(2,1)} %param.12) | data formatting | bytes 589824 | tf_op jit(solution)/shard_map/reshape | solution.py:283
  2.9 0.4 copy.30
  3.3 0.0 copy-start.2
  3.3 0.4 reshape.13.wn_ref
  3.8 0.5 %copy-done.2 = bf16[8,64,288]{2,1,0:T(8,128)(2,1)S(1)} copy-done((bf16[8,64,288]{2,1,0:T(8,128)(2,1)S(1)}, bf16[8,64,288]{2,1,0:T(8,128)(2,1)}, u32[]{:S(2)}) %copy-start.2) | copy-done | bytes 294936
  4.3 0.3 copy.31
  4.6 0.4 copy.32
  5.0 0.4 reshape.15
  5.5 0.0 copy-start
  5.5 0.0 copy-start.1
  5.5 0.2 copy.33.ww_ref
  5.8 0.8 %copy-done = bf16[512,512]{1,0:T(8,128)(2,1)S(1)} copy-done((bf16[512,512]{1,0:T(8,128)(2,1)S(1)}, bf16[512,512]{1,0:T(8,128)(2,1)}, u32[]{:S(2)}) %copy-start) | copy-done | bytes 524312
  6.5 0.0 copy-done.1
  6.6 41.7 %shard_map.91 = bf16[4,64,128]{2,1,0:T(8,128)(2,1)S(1)} custom-call(bf16[4,64,128]{2,1,0:T(8,128)(2,1)S(1)} %bitcast.12, f32[192,8]{1,0:T(8,128)S(1)} %bitcast.11, bf16[8,96,192]{2,1,0:T(8,128)(2,1)S(1)} %reshape.13.wn_ref, bf16[8,192,96]{2,1,0:T(8,128)(2,1)S(1)} %copy.33.ww_ref, bf16[256,256]{1,0:T(8,128)(2,1)S(1)} %copy-done.1, bf16[512,512]{1,0:T(8,128)(2,1)S(1)} %copy-done), custom_call_target="tpu_custom_call" | custom-call | tf_op jit(solution)/shard_map/pallas_call | solution.py:289
  48.2 0.7 %copy.34 = bf16[64,4,128]{2,1,0:T(4,128)(2,1)} copy(bf16[64,4,128]{2,0,1:T(8,128)(2,1)S(1)} %bitcast.13) | data formatting | bytes 131072 | tf_op jit(solution)/shard_map/transpose | solution.py:321
Async XLA Ops:
  0.0 0.9 %copy-start.3 = (f32[8,32]{1,0:T(8,128)S(1)}, f32[8,32]{1,0:T(8,128)}, u32[]{:S(2)}) copy-start(f32[8,32]{1,0:T(8,128)} %param.14) | copy-start | bytes 3076
  0.0 0.9 %copy-start.4 = (f32[8,32]{1,0:T(8,128)S(1)}, f32[8,32]{1,0:T(8,128)}, u32[]{:S(2)}) copy-start(f32[8,32]{1,0:T(8,128)} %param.13) | copy-start | bytes 3076
  0.0 0.9 %copy-start.5 = (f32[8,64]{1,0:T(8,128)S(1)}, f32[8,64]{1,0:T(8,128)}, u32[]{:S(2)}) copy-start(f32[8,64]{1,0:T(8,128)} %param.11) | copy-start | bytes 6148
  0.0 0.9 %copy-start.6 = (f32[8,64]{1,0:T(8,128)S(1)}, f32[8,64]{1,0:T(8,128)}, u32[]{:S(2)}) copy-start(f32[8,64]{1,0:T(8,128)} %param.10) | copy-start | bytes 6148
  3.3 1.0 %copy-start.2 = (bf16[8,64,288]{2,1,0:T(8,128)(2,1)S(1)}, bf16[8,64,288]{2,1,0:T(8,128)(2,1)}, u32[]{:S(2)}) copy-start(bf16[8,64,288]{2,1,0:T(8,128)(2,1)} %param.15) | copy-start | bytes 884740
  5.5 1.0 %copy-start = (bf16[512,512]{1,0:T(8,128)(2,1)S(1)}, bf16[512,512]{1,0:T(8,128)(2,1)}, u32[]{:S(2)}) copy-start(bf16[512,512]{1,0:T(8,128)(2,1)} %constant.5.clone.unpack_ref) | copy-start | bytes 1572868
  5.5 1.1 %copy-start.1 = (bf16[256,256]{1,0:T(8,128)(2,1)S(1)}, bf16[256,256]{1,0:T(8,128)(2,1)}, u32[]{:S(2)}) copy-start(bf16[256,256]{1,0:T(8,128)(2,1)} %constant.4.clone.pack_ref) | copy-start | bytes 393220

commit v2 on v1

--- a/solution.py
+++ b/solution.py
@@ -8,7 +8,7 @@
 from jax.experimental.pallas import tpu as pltpu
 from jax.sharding import PartitionSpec as P
 
-GROUPS = ((1, 1), (2, 2))
+GROUPS = ((1, 1), (2,), (2,))
 LANES = 128
 
 
@@ -47,20 +47,31 @@
     return parts[1] + low + high
 
 
+def shifts(value, dilation, lane):
+    width = lane.shape[-1]
+    low = jnp.where(lane < dilation, 0.0, pltpu.roll(value, dilation, 1))
+    high = jnp.where(lane >= width - dilation, 0.0, pltpu.roll(value, width - dilation, 1))
+    return low, value, high
+
+
 def network_kernel(
-    count, rounds, x_ref, params_ref, wn_ref, ww_ref, pack_ref, unpack_ref, out_ref, *scratch
+    count, rounds, x_ref, params_ref, raw_ref, ww_ref, pack_ref, unpack_ref, out_ref, *scratch
 ):
     rows, channels, width = x_ref.shape
-    mid = ww_ref.shape[2] // 3
+    blocks, mid = raw_ref.shape[:2]
     side = rows * count
     halves = rows * channels // LANES
     subs = LANES // channels
     pieces = rows * halves
     groups = len(GROUPS)
     tiles = scratch[: rounds * groups]
-    sent, got, stream_buf, hidden_buf, inner_buf = scratch[rounds * groups : rounds * groups + 5]
-    mirror_send, mirror_recv, halo_send, halo_recv = scratch[rounds * groups + 5 :]
+    sent, got, stream_buf, hidden_buf, inner_buf, wn_ref = scratch[rounds * groups :][:6]
+    mirror_send, mirror_recv, halo_send, halo_recv = scratch[rounds * groups + 6 :]
     me = lax.axis_index("row")
+
+    def wrapped(k):
+        t = me + k
+        return jnp.where(t >= count, t - count, t)
 
     barrier = pltpu.get_barrier_semaphore()
 
@@ -68,7 +79,7 @@
         pl.semaphore_signal(
             barrier,
             inc=1,
-            device_id={"row": lax.rem(me + k, count)},
+            device_id={"row": wrapped(k)},
             device_id_type=pl.DeviceIdType.MESH,
         )
         return carry
@@ -116,16 +127,27 @@
             pack(rd, stream)
 
         def send(k, carry):
-            mirror_copy(rd, lax.rem(me + k, count), me).start()
+            mirror_copy(rd, wrapped(k), me).start()
             return carry
 
         def receive(k, carry):
-            source = lax.rem(me + k, count)
+            source = wrapped(k)
             mirror_copy(rd, source, source).wait_recv()
             return carry
 
         lax.fori_loop(1, count, send, 0)
         got[rd, me] = sent[rd, me]
+        if rd == 0:
+            def reorder(b, carry):
+                raw = raw_ref[b]
+                for kx in range(3):
+                    taps = [(3 * ky + kx) * channels for ky in range(3)]
+                    wn_ref[b, kx * mid : (kx + 1) * mid] = jnp.concatenate(
+                        [raw[:, t : t + channels] for t in taps], axis=1
+                    )
+                return carry
+
+            lax.fori_loop(0, blocks, reorder, 0)
         lax.fori_loop(1, count, receive, 0)
 
         arrived = got[rd].astype(jnp.float32).reshape(count * pieces, LANES).T
@@ -164,12 +186,6 @@
                 def _():
                     halo_copy(k, reach - k, me + k).start()
 
-            for k in offsets:
-
-                @pl.when((me + k >= 0) & (me + k < count))
-                def _():
-                    halo_copy(k, reach + k, me + k).wait_recv()
-
             halo = 2 * sum(group)
             lo = reach * rows - halo
             hi = (reach + 1) * rows + halo
@@ -199,9 +215,19 @@
                 def load(e):
                     return tile[e // rows, e % rows] if bi == 0 else stream_buf[e]
 
-                for e in range(lo, hi):
-                    value = jnp.maximum(load(e).astype(jnp.float32) * scale_o + shift_o, 0.0)
-                    hidden_buf[e] = masked(value, e).astype(jnp.bfloat16)
+                own = range(reach * rows, (reach + 1) * rows)
+                outer = [e for e in range(lo, hi) if e not in own]
+                for part in (own, outer):
+                    if part is outer and bi == 0:
+                        for k in offsets:
+
+                            @pl.when((me + k >= 0) & (me + k < count))
+                            def _():
+                                halo_copy(k, reach + k, me + k).wait_recv()
+
+                    for e in part:
+                        value = jnp.maximum(load(e).astype(jnp.float32) * scale_o + shift_o, 0.0)
+                        hidden_buf[e] = masked(value, e).astype(jnp.bfloat16)
                 for e in range(lo + d, hi - d, 2):
                     both = jnp.concatenate(
                         [
@@ -218,7 +244,9 @@
                         ]
                         narrow = shifted_sum(parts, d, lane)
                         value = jnp.maximum(narrow * scale_i + shift_i, 0.0)
-                        inner_buf[e + i] = masked(value, e + i).astype(jnp.bfloat16)
+                        value = masked(value, e + i)
+                        for kx, part in enumerate(shifts(value, d, lane)):
+                            inner_buf[e + i, kx * mid : (kx + 1) * mid] = part.astype(jnp.bfloat16)
                 lo, hi = lo + 2 * d, hi - 2 * d
                 final = bi == len(group) - 1
                 stream = [None] * rows
@@ -232,11 +260,7 @@
                     )
                     y = jnp.dot(ww_ref[block], both, preferred_element_type=jnp.float32)
                     for i in range(2):
-                        parts = [
-                            y[kx * channels : (kx + 1) * channels, i * width : (i + 1) * width]
-                            for kx in range(3)
-                        ]
-                        widened = shifted_sum(parts, d, lane)
+                        widened = y[:, i * width : (i + 1) * width]
                         value = (load(e + i).astype(jnp.float32) + widened).astype(jnp.bfloat16)
                         if final:
                             stream[e + i - lo] = value
@@ -250,7 +274,7 @@
     for rd in range(rounds):
 
         def finish(k, carry):
-            target = lax.rem(me + k, count)
+            target = wrapped(k)
             mirror_copy(rd, target, me).wait_send()
             return carry
 
@@ -280,8 +304,6 @@
     halves = rows * channels // LANES
     pack, unpack = spread_constants(rows, channels, width)
     params = jnp.concatenate([gain_outer, bias_outer, gain_inner, bias_inner], axis=1).T
-    wn = w_narrow.reshape(blocks, mid, 3, 3, channels).transpose(0, 3, 1, 2, 4)
-    ww = w_widen.reshape(blocks, channels, 3, 3, mid).transpose(0, 3, 1, 2, 4)
     reaches = [-(-2 * sum(g) // rows) for g in GROUPS]
     tall = (2 * max(reaches) + 1) * rows
     phases = rounds * len(GROUPS)
@@ -301,7 +323,8 @@
             pltpu.VMEM((rounds, count, rows * halves, LANES), jnp.bfloat16),
             pltpu.VMEM((tall, channels, width), jnp.bfloat16),
             pltpu.VMEM((tall, channels, width), jnp.bfloat16),
-            pltpu.VMEM((tall, mid, width), jnp.bfloat16),
+            pltpu.VMEM((tall, 3 * mid, width), jnp.bfloat16),
+            pltpu.VMEM((blocks, 3 * mid, 3 * channels), jnp.bfloat16),
             dma((rounds, count)),
             dma((rounds, count)),
             dma((phases, 2 * max(reaches) + 1)),
@@ -313,8 +336,8 @@
     )(
         features_in.transpose(1, 0, 2),
         params,
-        wn.reshape(blocks, 3 * mid, 3 * channels),
-        ww.reshape(blocks, 3 * channels, 3 * mid),
+        w_narrow,
+        w_widen,
         pack,
         unpack,
     )

time: 49.2 us -> 49.5 us (level)
  the two profiles are of different devices: /device:TPU:5 before, /device:TPU:8 now
where the time goes in v2:
time: 49.5 us; the launch traced here: 49.2 us
  Pallas kernels  43.6 us (88%)
  local copies, waits for them, and re-layouts  4.65 us (9%)
  other arithmetic  0.85 us (2%)
    pallas_call x1, Pallas kernels, fused_body(): pl.pallas_call(functools.partial(network_kernel, count, rounds), out_shap...  43.6 us
    unnamed x9, local copies, waits for them, and re-layouts  3.86 us

profile of v2, /device:TPU:8, one launch (start us, length us, event | category | flops | bytes accessed | tf_op | source)
XLA Modules:
  0.0 49.2 jit_solution(12117706796810165152)
XLA Ops:
  0.0 0.0 copy-start.3
  0.0 0.8 %pad_maximum_fusion = f32[8,192]{1,0:T(8,128)S(1)} fusion(f32[8,32]{1,0:T(8,128)} %param.14, f32[8,32]{1,0:T(8,128)} %param.13, f32[8,64]{1,0:T(8,128)} %param.11, f32[8,64]{1,0:T(8,128)} %param.10), kind=kLoop, calls=%fused_computation.1 | loop fusion | flops 4608 | bytes 12288 | tf_op jit(solution)/shard_map/concatenate | solution.py:306
  0.8 0.9 %copy.20 = bf16[64,4,128]{2,0,1:T(8,128)(2,1)S(1)} copy(bf16[64,4,128]{2,1,0:T(4,128)(2,1)} %param.9) | data formatting | bytes 131072 | tf_op args[0]
  1.7 0.1 copy.17
  1.8 0.0 copy-done.3
  1.8 0.0 copy-start
  1.8 1.0 %copy-done = bf16[512,512]{1,0:T(8,128)(2,1)S(1)} copy-done((bf16[512,512]{1,0:T(8,128)(2,1)S(1)}, bf16[512,512]{1,0:T(8,128)(2,1)}, u32[]{:S(2)}) %copy-start) | copy-done | bytes 524312
  2.9 0.0 copy-start.1
  2.9 1.0 %copy-done.1 = bf16[8,64,288]{2,1,0:T(8,128)(2,1)S(1)} copy-done((bf16[8,64,288]{2,1,0:T(8,128)(2,1)S(1)}, bf16[8,64,288]{2,1,0:T(8,128)(2,1)}, u32[]{:S(2)}) %copy-start.1) | copy-done | bytes 294936
  3.9 0.0 copy-start.2
  3.9 1.0 %copy-done.2 = bf16[8,32,576]{2,1,0:T(8,128)(2,1)S(1)} copy-done((bf16[8,32,576]{2,1,0:T(8,128)(2,1)S(1)}, bf16[8,32,576]{2,1,0:T(8,128)(2,1)}, u32[]{:S(2)}) %copy-start.2) | copy-done | bytes 294936
  4.8 43.6 %shard_map.91 = bf16[4,64,128]{2,1,0:T(8,128)(2,1)S(1)} custom-call(bf16[4,64,128]{2,1,0:T(8,128)(2,1)S(1)} %bitcast.6, f32[192,8]{1,0:T(8,128)S(1)} %bitcast.5, bf16[8,32,576]{2,1,0:T(8,128)(2,1)S(1)} %copy-done.2, bf16[8,64,288]{2,1,0:T(8,128)(2,1)S(1)} %copy-done.1, bf16[256,256]{1,0:T(8,128)(2,1)S(1)} %copy-done.3, bf16[512,512]{1,0:T(8,128)(2,1)S(1)} %copy-done), custom_call_target="tpu_custom_call" | custom-call | tf_op jit(solution)/shard_map/pallas_call | solution.py:311
  48.5 0.7 %copy.18 = bf16[64,4,128]{2,1,0:T(4,128)(2,1)} copy(bf16[64,4,128]{2,0,1:T(8,128)(2,1)S(1)} %bitcast.7) | data formatting | bytes 131072 | tf_op jit(solution)/shard_map/transpose | solution.py:344
Async XLA Ops:
  0.0 1.8 %copy-start.3 = (bf16[256,256]{1,0:T(8,128)(2,1)S(1)}, bf16[256,256]{1,0:T(8,128)(2,1)}, u32[]{:S(2)}) copy-start(bf16[256,256]{1,0:T(8,128)(2,1)} %constant.4.clone.pack_ref) | copy-start | bytes 393220
  1.8 1.0 %copy-start = (bf16[512,512]{1,0:T(8,128)(2,1)S(1)}, bf16[512,512]{1,0:T(8,128)(2,1)}, u32[]{:S(2)}) copy-start(bf16[512,512]{1,0:T(8,128)(2,1)} %constant.5.clone.unpack_ref) | copy-start | bytes 1572868
  2.9 1.0 %copy-start.1 = (bf16[8,64,288]{2,1,0:T(8,128)(2,1)S(1)}, bf16[8,64,288]{2,1,0:T(8,128)(2,1)}, u32[]{:S(2)}) copy-start(bf16[8,64,288]{2,1,0:T(8,128)(2,1)} %ww_ref.1) | copy-start | bytes 884740
  3.9 1.0 %copy-start.2 = (bf16[8,32,576]{2,1,0:T(8,128)(2,1)S(1)}, bf16[8,32,576]{2,1,0:T(8,128)(2,1)}, u32[]{:S(2)}) copy-start(bf16[8,32,576]{2,1,0:T(8,128)(2,1)} %raw_ref.1) | copy-start | bytes 884740

commit v3 on v2

--- a/solution.py
+++ b/solution.py
@@ -37,7 +37,7 @@
     q = (r % subs) * (count * pieces) + j * pieces + xx * halves + r // subs
     unpack = np.zeros((subs * count * pieces, rows * width), np.float32)
     unpack[q, o] = 1
-    return jnp.asarray(pack, jnp.bfloat16), jnp.asarray(unpack, jnp.bfloat16)
+    return jnp.asarray(pack), jnp.asarray(unpack)
 
 
 def shifted_sum(parts, dilation, lane):
@@ -55,10 +55,19 @@
 
 
 def network_kernel(
-    count, rounds, x_ref, params_ref, raw_ref, ww_ref, pack_ref, unpack_ref, out_ref, *scratch
+    count, rounds, x_ref, *refs
 ):
     rows, channels, width = x_ref.shape
+    hbm, out_ref, scratch = refs[:8], refs[8], refs[9:]
+    held, held_sem, params_ref, scratch = scratch[:8], scratch[8], scratch[9], scratch[10:]
+    pack_ref, unpack_ref, raw_ref, ww_ref = held[:4]
     blocks, mid = raw_ref.shape[:2]
+    fetches = [
+        pltpu.make_async_copy(source, target, held_sem.at[i])
+        for i, (source, target) in enumerate(zip(hbm, held))
+    ]
+    for fetch in fetches:
+        fetch.start()
     side = rows * count
     halves = rows * channels // LANES
     subs = LANES // channels
@@ -104,7 +113,7 @@
             [jnp.concatenate(flat[h * per : (h + 1) * per], axis=0) for h in range(halves)], axis=1
         )
         packed = lax.dot_general(
-            pack_ref[...], cat, (((1,), (1,)), ((), ())), preferred_element_type=jnp.float32
+            pack_ref[...].astype(jnp.bfloat16), cat, (((1,), (1,)), ((), ())), preferred_element_type=jnp.float32
         )
         sent[rd] = packed.reshape(count, pieces, LANES).astype(jnp.bfloat16)
 
@@ -112,13 +121,24 @@
         return remote(
             sent.at[rd, target],
             got.at[rd, source],
-            mirror_send.at[rd, target],
-            mirror_recv.at[rd, source],
+            mirror_send.at[rd],
+            mirror_recv.at[rd],
             target,
+        )
+
+    def mirror_all(rd):
+        rest = pl.ds(0, count - 1)
+        return remote(
+            sent.at[rd, rest],
+            got.at[rd, rest],
+            mirror_send.at[rd],
+            mirror_recv.at[rd],
+            wrapped(1),
         )
 
     lane = lax.broadcasted_iota(jnp.int32, (1, width), 1)
     stream = [x_ref[r] for r in range(rows)]
+    fetches[0].wait()
     pack(0, stream)
     pl.semaphore_wait(barrier, count - 1)
 
@@ -130,14 +150,16 @@
             mirror_copy(rd, wrapped(k), me).start()
             return carry
 
-        def receive(k, carry):
-            source = wrapped(k)
-            mirror_copy(rd, source, source).wait_recv()
-            return carry
-
         lax.fori_loop(1, count, send, 0)
         got[rd, me] = sent[rd, me]
         if rd == 0:
+            for fetch in fetches[1:]:
+                fetch.wait()
+            outer = jnp.concatenate([held[4][...], held[5][...]], axis=1)
+            inner = jnp.concatenate([held[6][...], held[7][...]], axis=1)
+            params_ref[: 2 * channels] = outer.T
+            params_ref[2 * channels :] = inner.T
+
             def reorder(b, carry):
                 raw = raw_ref[b]
                 for kx in range(3):
@@ -148,13 +170,15 @@
                 return carry
 
             lax.fori_loop(0, blocks, reorder, 0)
-        lax.fori_loop(1, count, receive, 0)
+        mirror_all(rd).wait_recv()
 
         arrived = got[rd].astype(jnp.float32).reshape(count * pieces, LANES).T
         arrived = jnp.concatenate(
             [arrived[u * channels : (u + 1) * channels] for u in range(subs)], axis=1
         ).astype(jnp.bfloat16)
-        partner = jnp.dot(arrived, unpack_ref[...], preferred_element_type=jnp.float32)
+        partner = jnp.dot(
+            arrived, unpack_ref[...].astype(jnp.bfloat16), preferred_element_type=jnp.float32
+        )
         stream = [
             (
                 (stream[r].astype(jnp.float32) + partner[:, r * width : (r + 1) * width]) * 0.5
@@ -228,16 +252,16 @@
                     for e in part:
                         value = jnp.maximum(load(e).astype(jnp.float32) * scale_o + shift_o, 0.0)
                         hidden_buf[e] = masked(value, e).astype(jnp.bfloat16)
-                for e in range(lo + d, hi - d, 2):
+                for e, some in [(lo + d, hi - lo - 2 * d)]:
                     both = jnp.concatenate(
                         [
                             jnp.concatenate([hidden_buf[e + i + (ky - 1) * d] for ky in range(3)], axis=0)
-                            for i in range(2)
+                            for i in range(some)
                         ],
                         axis=1,
                     )
                     y = jnp.dot(wn_ref[block], both, preferred_element_type=jnp.float32)
-                    for i in range(2):
+                    for i in range(some):
                         parts = [
                             y[kx * mid : (kx + 1) * mid, i * width : (i + 1) * width]
                             for kx in range(3)
@@ -250,16 +274,16 @@
                 lo, hi = lo + 2 * d, hi - 2 * d
                 final = bi == len(group) - 1
                 stream = [None] * rows
-                for e in range(lo, hi, 2):
+                for e, some in [(lo, hi - lo)]:
                     both = jnp.concatenate(
                         [
                             jnp.concatenate([inner_buf[e + i + (ky - 1) * d] for ky in range(3)], axis=0)
-                            for i in range(2)
+                            for i in range(some)
                         ],
                         axis=1,
                     )
                     y = jnp.dot(ww_ref[block], both, preferred_element_type=jnp.float32)
-                    for i in range(2):
+                    for i in range(some):
                         widened = y[:, i * width : (i + 1) * width]
                         value = (load(e + i).astype(jnp.float32) + widened).astype(jnp.bfloat16)
                         if final:
@@ -272,13 +296,7 @@
         out_ref[r] = stream[r]
 
     for rd in range(rounds):
-
-        def finish(k, carry):
-            target = wrapped(k)
-            mirror_copy(rd, target, me).wait_send()
-            return carry
-
-        lax.fori_loop(1, count, finish, 0)
+        mirror_all(rd).wait_send()
         for gi in range(groups):
             phase = rd * groups + gi
             tile = tiles[phase]
@@ -303,7 +321,7 @@
     rounds = blocks // sum(len(g) for g in GROUPS)
     halves = rows * channels // LANES
     pack, unpack = spread_constants(rows, channels, width)
-    params = jnp.concatenate([gain_outer, bias_outer, gain_inner, bias_inner], axis=1).T
+    fetched = (pack, unpack, w_narrow, w_widen, gain_outer, bias_outer, gain_inner, bias_inner)
     reaches = [-(-2 * sum(g) // rows) for g in GROUPS]
     tall = (2 * max(reaches) + 1) * rows
     phases = rounds * len(GROUPS)
@@ -311,9 +329,12 @@
     out = pl.pallas_call(
         functools.partial(network_kernel, count, rounds),
         out_shape=jax.ShapeDtypeStruct((rows, channels, width), jnp.bfloat16),
-        in_specs=[pl.BlockSpec(memory_space=pltpu.VMEM)] * 6,
+        in_specs=[pl.BlockSpec(memory_space=pltpu.VMEM)]
+        + [pl.BlockSpec(memory_space=pltpu.HBM)] * len(fetched),
         out_specs=pl.BlockSpec(memory_space=pltpu.VMEM),
-        scratch_shapes=[
+        scratch_shapes=[pltpu.VMEM(a.shape, a.dtype) for a in fetched]
+        + [dma((len(fetched),)), pltpu.VMEM((2 * (channels + mid), blocks), jnp.float32)]
+        + [
             pltpu.VMEM((2 * r + 1, rows, channels, width), jnp.bfloat16)
             for _ in range(rounds)
             for r in reaches
@@ -325,21 +346,17 @@
             pltpu.VMEM((tall, channels, width), jnp.bfloat16),
             pltpu.VMEM((tall, 3 * mid, width), jnp.bfloat16),
             pltpu.VMEM((blocks, 3 * mid, 3 * channels), jnp.bfloat16),
-            dma((rounds, count)),
-            dma((rounds, count)),
+            dma((rounds,)),
+            dma((rounds,)),
             dma((phases, 2 * max(reaches) + 1)),
             dma((phases, 2 * max(reaches) + 1)),
         ],
         compiler_params=pltpu.CompilerParams(
-            collective_id=0, has_side_effects=True, vmem_limit_bytes=32 * 1024 * 1024
+            collective_id=0, has_side_effects=True, vmem_limit_bytes=60 * 1024 * 1024
         ),
     )(
         features_in.transpose(1, 0, 2),
-        params,
-        w_narrow,
-        w_widen,
-        pack,
-        unpack,
+        *fetched,
     )
     return out.transpose(1, 0, 2)
 

time: 49.5 us -> 46.6 us (0.941)
  local copies, waits for them, and re-layouts: 4.65 us -> 3 us
  other arithmetic: 0.85 us -> 0 us
    unnamed x9 -> x1, local copies, waits for them, and re-layouts: 3.86 us -> 1.48 us
    concatenate x1 -> x0, other arithmetic: 0.85 us -> none  [fused_body(): jnp.concatenate([gain_outer, bias_outer, gain_inner, bias_inner], axis=1)]
    transpose x1, local copies, waits for them, and re-layouts: 0.68 us -> 1.52 us  [fused_body(): return out.transpose(1, 0, 2)]
where the time goes in v3:
time: 46.6 us; the launch traced here: 46.3 us
  Pallas kernels  43.3 us (93%)
  local copies, waits for them, and re-layouts  3 us (6%)
    pallas_call x1, Pallas kernels, fused_body(): pl.pallas_call(functools.partial(network_kernel, count, rounds), out_shap...  43.3 us
    transpose x1, local copies, waits for them, and re-layouts, fused_body(): return out.transpose(1, 0, 2)  1.52 us
    unnamed x1, local copies, waits for them, and re-layouts  1.48 us

profile of v3, /device:TPU:8, one launch (start us, length us, event | category | flops | bytes accessed | tf_op | source)
XLA Modules:
  0.0 46.3 jit_solution(4806686349709712018)
XLA Ops:
  0.0 1.5 %copy.13 = bf16[64,4,128]{2,0,1:T(8,128)(2,1)} copy(bf16[64,4,128]{2,1,0:T(4,128)(2,1)} %param.9) | data formatting | bytes 131072 | tf_op args[0]
  1.5 43.3 %shard_map.91 = bf16[4,64,128]{2,1,0:T(8,128)(2,1)} custom-call(bf16[4,64,128]{2,1,0:T(8,128)(2,1)} %bitcast.5, f32[256,256]{1,0:T(8,128)} %constant.4.clone.refs_0_, f32[512,512]{1,0:T(8,128)} %constant.5.clone.refs_1_, bf16[8,32,576]{2,1,0:T(8,128)(2,1)} %refs_2_.1, bf16[8,64,288]{2,1,0:T(8,128)(2,1)} %refs_3_.1, f32[8,64]{1,0:T(8,128)} %refs_4_.1, ...), custom_call_target="tpu_custom_call" | custom-call | tf_op jit(solution)/shard_map/pallas_call | solution.py:329
  44.8 1.5 %copy.11 = bf16[64,4,128]{2,1,0:T(4,128)(2,1)} copy(bf16[64,4,128]{2,0,1:T(8,128)(2,1)} %bitcast.4) | data formatting | bytes 131072 | tf_op jit(solution)/shard_map/transpose | solution.py:361

commit v4 on v3

--- a/solution.py
+++ b/solution.py
@@ -57,9 +57,10 @@
 def network_kernel(
     count, rounds, x_ref, *refs
 ):
-    rows, channels, width = x_ref.shape
+    channels, rows, width = x_ref.shape
     hbm, out_ref, scratch = refs[:8], refs[8], refs[9:]
-    held, held_sem, params_ref, scratch = scratch[:8], scratch[8], scratch[9], scratch[10:]
+    held, held_sem, params_ref, x_wide = scratch[:8], scratch[8], scratch[9], scratch[10]
+    scratch = scratch[11:]
     pack_ref, unpack_ref, raw_ref, ww_ref = held[:4]
     blocks, mid = raw_ref.shape[:2]
     fetches = [
@@ -84,16 +85,18 @@
 
     barrier = pltpu.get_barrier_semaphore()
 
-    def greet(k, carry):
+    far_first = sorted(range(1, count), key=lambda k: -min(k, count - k))
+
+    def greet(k):
         pl.semaphore_signal(
             barrier,
             inc=1,
             device_id={"row": wrapped(k)},
             device_id_type=pl.DeviceIdType.MESH,
         )
-        return carry
-
-    lax.fori_loop(1, count, greet, 0)
+
+    for k in far_first:
+        greet(k)
     for phase in range(rounds * groups):
         tile = tiles[phase]
         reach = tile.shape[0] // 2
@@ -137,7 +140,8 @@
         )
 
     lane = lax.broadcasted_iota(jnp.int32, (1, width), 1)
-    stream = [x_ref[r] for r in range(rows)]
+    x_wide[...] = x_ref[...].astype(jnp.float32)
+    stream = [x_wide[:, r, :].astype(jnp.bfloat16) for r in range(rows)]
     fetches[0].wait()
     pack(0, stream)
     pl.semaphore_wait(barrier, count - 1)
@@ -146,11 +150,8 @@
         if rd:
             pack(rd, stream)
 
-        def send(k, carry):
+        for k in far_first:
             mirror_copy(rd, wrapped(k), me).start()
-            return carry
-
-        lax.fori_loop(1, count, send, 0)
         got[rd, me] = sent[rd, me]
         if rd == 0:
             for fetch in fetches[1:]:
@@ -334,6 +335,7 @@
         out_specs=pl.BlockSpec(memory_space=pltpu.VMEM),
         scratch_shapes=[pltpu.VMEM(a.shape, a.dtype) for a in fetched]
         + [dma((len(fetched),)), pltpu.VMEM((2 * (channels + mid), blocks), jnp.float32)]
+        + [pltpu.VMEM(features_in.shape, jnp.float32)]
         + [
             pltpu.VMEM((2 * r + 1, rows, channels, width), jnp.bfloat16)
             for _ in range(rounds)
@@ -355,7 +357,7 @@
             collective_id=0, has_side_effects=True, vmem_limit_bytes=60 * 1024 * 1024
         ),
     )(
-        features_in.transpose(1, 0, 2),
+        features_in,
         *fetched,
     )
     return out.transpose(1, 0, 2)

time: 46.6 us -> 44.7 us (0.959)
  local copies, waits for them, and re-layouts: 3 us -> 1.52 us
    unnamed x1 -> x0, local copies, waits for them, and re-layouts: 1.48 us -> none
where the time goes in v4:
time: 44.7 us; the launch traced here: 44.5 us
  Pallas kernels  42.9 us (96%)
  local copies, waits for them, and re-layouts  1.52 us (3%)
    pallas_call x1, Pallas kernels, fused_body(): pl.pallas_call(functools.partial(network_kernel, count, rounds), out_shap...  42.9 us
    transpose x1, local copies, waits for them, and re-layouts, fused_body(): return out.transpose(1, 0, 2)  1.52 us

profile of v4, /device:TPU:8, one launch (start us, length us, event | category | flops | bytes accessed | tf_op | source)
XLA Modules:
  0.0 44.5 jit_solution(18208615564183230767)
XLA Ops:
  0.0 42.9 %shard_map.91 = bf16[4,64,128]{2,1,0:T(8,128)(2,1)} custom-call(bf16[64,4,128]{2,1,0:T(4,128)(2,1)} %x_ref.1, f32[256,256]{1,0:T(8,128)} %constant.4.clone.refs_0_, f32[512,512]{1,0:T(8,128)} %constant.5.clone.refs_1_, bf16[8,32,576]{2,1,0:T(8,128)(2,1)} %refs_2_.1, bf16[8,64,288]{2,1,0:T(8,128)(2,1)} %refs_3_.1, f32[8,64]{1,0:T(8,128)} %refs_4_.1, ...), custom_call_target="tpu_custom_call" | custom-call | tf_op jit(solution)/shard_map/pallas_call | solution.py:330
  42.9 1.5 %copy.10 = bf16[64,4,128]{2,1,0:T(4,128)(2,1)} copy(bf16[64,4,128]{2,0,1:T(8,128)(2,1)} %bitcast.1) | data formatting | bytes 131072 | tf_op jit(solution)/shard_map/transpose | solution.py:363

commit v5 on v4

--- a/solution.py
+++ b/solution.py
@@ -74,9 +74,9 @@
     subs = LANES // channels
     pieces = rows * halves
     groups = len(GROUPS)
-    tiles = scratch[: rounds * groups]
-    sent, got, stream_buf, hidden_buf, inner_buf, wn_ref = scratch[rounds * groups :][:6]
-    mirror_send, mirror_recv, halo_send, halo_recv = scratch[rounds * groups + 6 :]
+    tiles = scratch[:groups]
+    sent, got, stream_buf, hidden_buf, inner_buf, wn_ref = scratch[groups:][:6]
+    mirror_send, mirror_recv, halo_send, halo_recv = scratch[groups + 6 :]
     me = lax.axis_index("row")
 
     def wrapped(k):
@@ -97,8 +97,8 @@
 
     for k in far_first:
         greet(k)
-    for phase in range(rounds * groups):
-        tile = tiles[phase]
+    for rd, gi in [(rd, gi) for rd in range(rounds) for gi in range(groups)]:
+        tile = tiles[gi].at[rd]
         reach = tile.shape[0] // 2
         for k in range(1, reach + 1):
             for sign in (-1, 1):
@@ -143,23 +143,26 @@
     x_wide[...] = x_ref[...].astype(jnp.float32)
     stream = [x_wide[:, r, :].astype(jnp.bfloat16) for r in range(rows)]
     fetches[0].wait()
-    pack(0, stream)
     pl.semaphore_wait(barrier, count - 1)
-
-    for rd in range(rounds):
-        if rd:
-            pack(rd, stream)
-
+    for r in range(rows):
+        stream_buf[r] = stream[r]
+
+    def one_round(rd, carry):
+        stream = [stream_buf[r] for r in range(rows)]
+        pack(rd, stream)
         for k in far_first:
             mirror_copy(rd, wrapped(k), me).start()
         got[rd, me] = sent[rd, me]
-        if rd == 0:
+
+        @pl.when(rd == 0)
+        def _():
             for fetch in fetches[1:]:
                 fetch.wait()
             outer = jnp.concatenate([held[4][...], held[5][...]], axis=1)
             inner = jnp.concatenate([held[6][...], held[7][...]], axis=1)
-            params_ref[: 2 * channels] = outer.T
-            params_ref[2 * channels :] = inner.T
+            columns = jnp.concatenate([outer.T, inner.T], axis=0)
+            for b in range(blocks):
+                params_ref[b] = jnp.broadcast_to(columns[:, b : b + 1], params_ref.shape[1:])
 
             def reorder(b, carry):
                 raw = raw_ref[b]
@@ -190,7 +193,7 @@
         block = rd * sum(len(g) for g in GROUPS)
         for gi, group in enumerate(GROUPS):
             phase = rd * groups + gi
-            tile = tiles[phase]
+            tile = tiles[gi].at[rd]
             reach = tile.shape[0] // 2
             for r in range(rows):
                 tile[reach, r] = stream[r]
@@ -228,9 +231,7 @@
             for bi, d in enumerate(group):
 
                 def param(start, size):
-                    return jnp.broadcast_to(
-                        params_ref[start : start + size, block : block + 1], (size, width)
-                    )
+                    return params_ref[block, start : start + size]
 
                 scale_o = param(0, channels)
                 shift_o = param(channels, channels)
@@ -292,15 +293,19 @@
                         else:
                             stream_buf[e + i] = value
                 block += 1
-
+        for r in range(rows):
+            stream_buf[r] = stream[r]
+        return carry
+
+    lax.fori_loop(0, rounds, one_round, 0)
     for r in range(rows):
-        out_ref[r] = stream[r]
+        out_ref[r] = stream_buf[r]
 
     for rd in range(rounds):
         mirror_all(rd).wait_send()
         for gi in range(groups):
             phase = rd * groups + gi
-            tile = tiles[phase]
+            tile = tiles[gi].at[rd]
             reach = tile.shape[0] // 2
             for k in [s * k for k in range(1, reach + 1) for s in (-1, 1)]:
 
@@ -334,11 +339,10 @@
         + [pl.BlockSpec(memory_space=pltpu.HBM)] * len(fetched),
         out_specs=pl.BlockSpec(memory_space=pltpu.VMEM),
         scratch_shapes=[pltpu.VMEM(a.shape, a.dtype) for a in fetched]
-        + [dma((len(fetched),)), pltpu.VMEM((2 * (channels + mid), blocks), jnp.float32)]
+        + [dma((len(fetched),)), pltpu.VMEM((blocks, 2 * (channels + mid), width), jnp.float32)]
         + [pltpu.VMEM(features_in.shape, jnp.float32)]
         + [
-            pltpu.VMEM((2 * r + 1, rows, channels, width), jnp.bfloat16)
-            for _ in range(rounds)
+            pltpu.VMEM((rounds, 2 * r + 1, rows, channels, width), jnp.bfloat16)
             for r in reaches
         ]
         + [

time: 44.7 us -> 45 us (level)
  no operation moved by 1% of the time
where the time goes in v5:
time: 45 us; the launch traced here: 44.8 us
  Pallas kernels  43.3 us (96%)
  local copies, waits for them, and re-layouts  1.52 us (3%)
    pallas_call x1, Pallas kernels, fused_body(): pl.pallas_call(functools.partial(network_kernel, count, rounds), out_shap...  43.3 us
    transpose x1, local copies, waits for them, and re-layouts, fused_body(): return out.transpose(1, 0, 2)  1.52 us

profile of v5, /device:TPU:8, one launch (start us, length us, event | category | flops | bytes accessed | tf_op | source)
XLA Modules:
  0.0 44.8 jit_solution(543811560075039529)
XLA Ops:
  0.0 43.3 %shard_map.91 = bf16[4,64,128]{2,1,0:T(8,128)(2,1)} custom-call(bf16[64,4,128]{2,1,0:T(4,128)(2,1)} %x_ref.1, f32[256,256]{1,0:T(8,128)} %constant.4.clone.refs_0_, f32[512,512]{1,0:T(8,128)} %constant.5.clone.refs_1_, bf16[8,32,576]{2,1,0:T(8,128)(2,1)} %refs_2_.1, bf16[8,64,288]{2,1,0:T(8,128)(2,1)} %refs_3_.1, f32[8,64]{1,0:T(8,128)} %refs_4_.1, ...), custom_call_target="tpu_custom_call" | custom-call | tf_op jit(solution)/shard_map/pallas_call | solution.py:335
  43.3 1.5 %copy.10 = bf16[64,4,128]{2,1,0:T(4,128)(2,1)} copy(bf16[64,4,128]{2,0,1:T(8,128)(2,1)} %bitcast.1) | data formatting | bytes 131072 | tf_op jit(solution)/shard_map/transpose | solution.py:367

commit v6 on v4

--- a/solution.py
+++ b/solution.py
@@ -8,7 +8,7 @@
 from jax.experimental.pallas import tpu as pltpu
 from jax.sharding import PartitionSpec as P
 
-GROUPS = ((1, 1), (2,), (2,))
+GROUPS = ((1, 1), (2, 2))
 LANES = 128
 
 
@@ -240,11 +240,12 @@
                 def load(e):
                     return tile[e // rows, e % rows] if bi == 0 else stream_buf[e]
 
-                own = range(reach * rows, (reach + 1) * rows)
-                outer = [e for e in range(lo, hi) if e not in own]
-                for part in (own, outer):
-                    if part is outer and bi == 0:
-                        for k in offsets:
+                for far in range(reach + 1):
+                    part = [
+                        e for e in range(lo, hi) if abs(e // rows - reach) == far
+                    ]
+                    if far and bi == 0:
+                        for k in (-far, far):
 
                             @pl.when((me + k >= 0) & (me + k < count))
                             def _():

time: 44.7 us -> 43 us (0.962)
  the two profiles are of different devices: /device:TPU:8 before, /device:TPU:5 now
where the time goes in v6:
time: 43 us; the launch traced here: 42.8 us
  Pallas kernels  41.3 us (96%)
  local copies, waits for them, and re-layouts  1.52 us (4%)
    pallas_call x1, Pallas kernels, fused_body(): pl.pallas_call(functools.partial(network_kernel, count, rounds), out_shap...  41.3 us
    transpose x1, local copies, waits for them, and re-layouts, fused_body(): return out.transpose(1, 0, 2)  1.52 us

profile of v6, /device:TPU:5, one launch (start us, length us, event | category | flops | bytes accessed | tf_op | source)
XLA Modules:
  0.0 42.8 jit_solution(8710692329734221176)
XLA Ops:
  0.0 41.3 %shard_map.91 = bf16[4,64,128]{2,1,0:T(8,128)(2,1)} custom-call(bf16[64,4,128]{2,1,0:T(4,128)(2,1)} %x_ref.1, f32[256,256]{1,0:T(8,128)} %constant.4.clone.refs_0_, f32[512,512]{1,0:T(8,128)} %constant.5.clone.refs_1_, bf16[8,32,576]{2,1,0:T(8,128)(2,1)} %refs_2_.1, bf16[8,64,288]{2,1,0:T(8,128)(2,1)} %refs_3_.1, f32[8,64]{1,0:T(8,128)} %refs_4_.1, ...), custom_call_target="tpu_custom_call" | custom-call | tf_op jit(solution)/shard_map/pallas_call | solution.py:331
  41.3 1.5 %copy.10 = bf16[64,4,128]{2,1,0:T(4,128)(2,1)} copy(bf16[64,4,128]{2,0,1:T(8,128)(2,1)} %bitcast.1) | data formatting | bytes 131072 | tf_op jit(solution)/shard_map/transpose | solution.py:364
